TPU v7x, 128 devices: a whole 4x4x4 slice. The times are simulated.
128 devices in a mesh: blk: 16 (over y, z_hi, core), fsdp: 8 (over z_lo, x).
Axes of the slice: x: 4, y: 4, z: 4 (z_hi: 2, z_lo: 2; z = z_hi * 2 + z_lo), core: 2. Of those that a mesh axis runs over, the one named last changes fastest.
Arguments:
- x_forward: bfloat16 [32768, 4096], P(('blk', 'fsdp'))
- seg_forward: int32 [128, 256], P(('blk', 'fsdp')), may hold values from 0 to 3, never falling along the last dimension, each value on 1 to 128 neighbouring positions
- x_saved: bfloat16 [32768, 4096], P(('blk', 'fsdp'))
- x_earlier: bfloat16 [32768, 4096], P(('blk', 'fsdp'))
- cotangent: bfloat16 [32768, 4096], P(('blk', 'fsdp')), may hold values from -0.119628906 to 0.119628906
- seg_backward: int32 [128, 256], P(('blk', 'fsdp')), may hold values from 0 to 3, never falling along the last dimension, each value on 1 to 128 neighbouring positions
- gain: bfloat16 [16, 4096], P('blk', 'fsdp'), may hold values from 0.25 to 1.75
- qkv: bfloat16 [16, 4096, 768], P('blk', 'fsdp')
- proj: bfloat16 [16, 512, 4096], P('blk', None, 'fsdp'), may hold values from -0.25 to 0.25
- sum_gain: float32 [16, 4096], P('blk', 'fsdp'), may hold values from -6 to 6
- sum_qkv: float32 [16, 4096, 768], P('blk', 'fsdp'), may hold values from -6 to 6
- sum_proj: float32 [16, 512, 4096], P('blk', None, 'fsdp'), may hold values from -6 to 6
Outputs:
- hidden_out: bfloat16 [32768, 4096], P(('blk', 'fsdp'))
- new_sum_gain: float32 [16, 4096], P('blk', 'fsdp')
- new_sum_qkv: float32 [16, 4096, 768], P('blk', 'fsdp')
- new_sum_proj: float32 [16, 512, 4096], P('blk', None, 'fsdp')
Inputs may be any that keep to these rules, and one draw needn't show every extreme that they name: `seg_forward`: each row of ids never falls along the micro-batch. `seg_backward`: each row of ids never falls along the micro-batch.
All inputs are finite; a program needn't handle non-finite values.
Results may differ from a plain program's by a relative error of at most 0.018.
The roundings to bfloat16 on the way count: a program that leaves them out, or rounds other values in their place, can miss the bound.
Values may be sent and summed in bfloat16 or wider, within the bound.
A program may use at most 192 MiB of HBM per device.

v0:
```python
import math

import jax
import jax.numpy as jnp
from jax import lax
from jax.sharding import PartitionSpec as P

HEADS = 4
HEAD_DIM = 128


def sent_together(arrays, axis, dim, along):
    widths = [math.prod(a.shape[along:]) for a in arrays]
    both = jnp.concatenate(
        [a.reshape(*a.shape[:along], w) for a, w in zip(arrays, widths)], axis=along
    )
    result = lax.psum_scatter(both, axis, scatter_dimension=dim, tiled=True)
    blocks = jnp.split(result, [sum(widths[:k]) for k in range(1, len(widths))], axis=along)
    return tuple(
        (b.reshape(*result.shape[:along], *a.shape[along:]) for a, b in zip(arrays, blocks))
    )


def shifted(value, axis, steps):
    count = lax.axis_size(axis)
    pairs = [(source, (source + steps) % count) for source in range(count)]
    return lax.ppermute(value, axis, pairs)


def attention_mask(segments):
    count = segments.shape[0]
    row_ids = lax.broadcasted_iota(jnp.int32, (count, count), 0)
    col_ids = lax.broadcasted_iota(jnp.int32, (count, count), 1)
    return (col_ids <= row_ids) & (segments[:, None] == segments[None, :])


def layer_parts(tokens, segments, norm_gain, qkv_weight):
    count = tokens.shape[0]
    att_width = HEADS * HEAD_DIM
    wide_rows = tokens.astype(jnp.float32)
    inv_rms = lax.rsqrt(jnp.mean(wide_rows * wide_rows, axis=1, keepdims=True) + 1e-05)
    normed = (wide_rows * inv_rms * norm_gain.astype(jnp.float32)[None, :]).astype(jnp.bfloat16)
    projected = jnp.dot(normed, qkv_weight, preferred_element_type=jnp.float32).astype(jnp.bfloat16)
    queries = projected[:, :att_width].reshape(count, HEADS, HEAD_DIM)
    key_rows = projected[:, att_width : att_width + HEAD_DIM]
    values = projected[:, att_width + HEAD_DIM :]
    score_scale = HEAD_DIM ** (-0.5)
    scores = (
        jnp.einsum("thd,sd->hts", queries, key_rows, preferred_element_type=jnp.float32)
        * score_scale
    )
    allowed = attention_mask(segments)[None]
    scores = jnp.where(allowed, scores, -1e30)
    row_max = jnp.max(scores, axis=2, keepdims=True)
    expo = jnp.where(allowed, jnp.exp(scores - row_max), 0.0)
    attn_probs = expo / jnp.sum(expo, axis=2, keepdims=True)
    attn_low = attn_probs.astype(jnp.bfloat16)
    attended = jnp.einsum("hts,sd->thd", attn_low, values, preferred_element_type=jnp.float32)
    attended = attended.reshape(count, att_width).astype(jnp.bfloat16)
    return (wide_rows, inv_rms, normed, queries, key_rows, values, attn_probs, attn_low, attended)


def layer_forward(tokens, segments, layer_weights):
    norm_gain, qkv_weight, proj_weight = layer_weights
    pieces_all = layer_parts(tokens, segments, norm_gain, qkv_weight)
    branch_out = jnp.dot(pieces_all[8], proj_weight, preferred_element_type=jnp.float32)
    return (pieces_all[0] + branch_out).astype(jnp.bfloat16)


def layer_backward(tokens, segments, layer_weights, upstream, with_input):
    norm_gain, qkv_weight, proj_weight = layer_weights
    wide_rows, inv_rms, normed, queries, key_rows, values, attn_probs, attn_low, attended = (
        layer_parts(tokens, segments, norm_gain, qkv_weight)
    )
    count = tokens.shape[0]
    d_att = lax.dot_general(
        upstream, proj_weight, (((1,), (1,)), ((), ())), preferred_element_type=jnp.float32
    ).astype(jnp.bfloat16)
    grad_proj = lax.dot_general(
        attended, upstream, (((0,), (0,)), ((), ())), preferred_element_type=jnp.float32
    )
    d_heads = d_att.reshape(count, HEADS, HEAD_DIM)
    d_probs = jnp.einsum("thd,sd->hts", d_heads, values, preferred_element_type=jnp.float32)
    grad_values = jnp.einsum("hts,thd->sd", attn_low, d_heads, preferred_element_type=jnp.float32)
    row_inner = jnp.sum(d_probs * attn_probs, axis=2, keepdims=True)
    d_scores = (attn_probs * (d_probs - row_inner) * HEAD_DIM ** (-0.5)).astype(jnp.bfloat16)
    grad_queries = jnp.einsum(
        "hts,sd->thd", d_scores, key_rows, preferred_element_type=jnp.float32
    ).reshape(count, HEADS * HEAD_DIM)
    grad_keys = jnp.einsum("hts,thd->sd", d_scores, queries, preferred_element_type=jnp.float32)
    d_projected = jnp.concatenate([grad_queries, grad_keys, grad_values], axis=1).astype(
        jnp.bfloat16
    )
    grad_qkv = lax.dot_general(
        normed, d_projected, (((0,), (0,)), ((), ())), preferred_element_type=jnp.float32
    )
    d_normed = lax.dot_general(
        d_projected, qkv_weight, (((1,), (1,)), ((), ())), preferred_element_type=jnp.float32
    )
    grad_gain = jnp.sum(d_normed * wide_rows * inv_rms, axis=0)
    grad_terms = (grad_gain, grad_qkv, grad_proj)
    if not with_input:
        return (grad_terms, upstream)
    scaled = d_normed * norm_gain.astype(jnp.float32)[None, :]
    d_wide = inv_rms * scaled - wide_rows * inv_rms**3 * jnp.mean(
        scaled * wide_rows, axis=1, keepdims=True
    )
    d_tokens = (upstream.astype(jnp.float32) + d_wide).astype(jnp.bfloat16)
    return (grad_terms, d_tokens)


def gather_layer(gain_piece, qkv_piece, proj_piece):
    gathered = (
        lax.all_gather(gain_piece, "fsdp", axis=1, tiled=True),
        lax.all_gather(qkv_piece, "fsdp", axis=1, tiled=True),
        lax.all_gather(proj_piece, "fsdp", axis=2, tiled=True),
    )
    return (gathered[0][0], gathered[1][0], gathered[2][0])


def reduce_terms(grad_terms):
    return (
        *tuple(
            (
                part.astype(jnp.float32)
                for part in sent_together(
                    (
                        grad_terms[0][None].astype(jnp.bfloat16),
                        grad_terms[1][None].astype(jnp.bfloat16),
                    ),
                    "fsdp",
                    1,
                    2,
                )
            )
        ),
        lax.psum_scatter(
            grad_terms[2][None].astype(jnp.bfloat16), "fsdp", scatter_dimension=2, tiled=True
        ).astype(jnp.float32),
    )


def body(
    x_forward,
    seg_forward,
    x_saved,
    x_earlier,
    cotangent,
    seg_backward,
    gain,
    qkv,
    proj,
    sum_gain,
    sum_qkv,
    sum_proj,
):
    ids_fwd = seg_forward[0]
    ids_bwd = seg_backward[0]
    layer_now = gather_layer(gain, qkv, proj)
    hidden = layer_forward(x_forward, ids_fwd, layer_now)
    terms_one, d_hidden = layer_backward(x_saved, ids_bwd, layer_now, cotangent, True)
    sums_one = reduce_terms(terms_one)
    carried = (
        shifted((sum_gain + sums_one[0]).astype(jnp.bfloat16), "blk", 1).astype(jnp.float32),
        shifted((sum_qkv + sums_one[1]).astype(jnp.bfloat16), "blk", 1).astype(jnp.float32),
        shifted((sum_proj + sums_one[2]).astype(jnp.bfloat16), "blk", 1).astype(jnp.float32),
    )
    moved = shifted((gain, qkv, proj), "blk", 1)
    layer_next = gather_layer(moved[0], moved[1], moved[2])
    result = layer_forward(hidden, ids_fwd, layer_next)
    terms_two, unused = layer_backward(x_earlier, ids_bwd, layer_next, d_hidden, False)
    sums_two = reduce_terms(terms_two)
    return (result, carried[0] + sums_two[0], carried[1] + sums_two[1], carried[2] + sums_two[2])


def solution(mesh):
    in_specs = (
        P(("blk", "fsdp"), None),
        P(("blk", "fsdp"), None),
        P(("blk", "fsdp"), None),
        P(("blk", "fsdp"), None),
        P(("blk", "fsdp"), None),
        P(("blk", "fsdp"), None),
        P("blk", "fsdp"),
        P("blk", "fsdp", None),
        P("blk", None, "fsdp"),
        P("blk", "fsdp"),
        P("blk", "fsdp", None),
        P("blk", None, "fsdp"),
    )
    out_specs = (
        P(("blk", "fsdp"), None),
        P("blk", "fsdp"),
        P("blk", "fsdp", None),
        P("blk", None, "fsdp"),
    )
    return jax.shard_map(body, mesh=mesh, in_specs=in_specs, out_specs=out_specs, check_vma=False)
```

profile of v0, /device:TPU:0, one launch (start us, length us, event | category | flops | bytes accessed | tf_op | source)
XLA Modules:
  0.0 539.3 jit_solution(12380102963807280710)
XLA Ops:
  8.8 15.7 %collective-permute-done.1 = bf16[1,512,768]{2,1,0:T(8,128)(2,1)S(1)} collective-permute-done((bf16[1,512,768]{2,1,0:T(8,128)(2,1)}, bf16[1,512,768]{2,1,0:T(8,128)(2,1)S(1)}, u32[]{:S(2)}, u32[]{:S(2)}) %collective-permute-start.1) | collective-permute-done | bytes 786464 | tf_op jit(solution)/shard_map/ppermute | solution.py:27
  25.6 18.0 %collective-permute-done.2 = bf16[1,512,512]{2,1,0:T(8,128)(2,1)S(1)} collective-permute-done((bf16[1,512,512]{2,1,0:T(8,128)(2,1)}, bf16[1,512,512]{2,1,0:T(8,128)(2,1)S(1)}, u32[]{:S(2)}, u32[]{:S(2)}) %collective-permute-start.2) | collective-permute-done | bytes 524320 | tf_op jit(solution)/shard_map/ppermute | solution.py:27
  44.5 63.2 %all_gather.18 = bf16[1,4096]{1,0:T(2,128)(2,1)S(1)} all-gather(bf16[1,512]{1,0:T(2,128)(2,1)} %param.18), channel_id=1, replica_groups=mesh['blk'=16,'fsdp'=8] {'fsdp'}, dimensions={1}, use_global_device_ids=true | all-gather | bytes 9216 | tf_op jit(solution)/shard_map/all_gather | solution.py:114
  107.7 2.1 fusion.38
  110.6 4.7 fusion.101
  115.5 1.5 fusion.206
  117.8 4.9 fusion.20
  123.0 20.2 %all-gather.7.cloned.1.call-done = bf16[1,512,4096]{2,1,0:T(8,128)(2,1)} async-done(((bf16[1,512,512]{2,1,0:T(8,128)(2,1)}), bf16[1,512,4096]{2,1,0:T(8,128)(2,1)}) %all-gather.7.cloned.1.call-update) | async-done | bytes 4194320 | tf_op jit(solution)/shard_map/all_gather | solution.py:116
  143.1 4.1 fusion.107
  148.5 2.2 fusion.113
  150.7 2.8 convolution_convert_fusion.7
  153.5 1.8 fusion.114
  155.3 7.3 %fusion.42 = (bf16[4096]{0:T(1024)(128)(2,1)S(1)}, f32[256]{0:T(256)S(1)}, f32[256,4096]{1,0:T(8,128)}) fusion(bf16[256,4096]{1,0:T(8,128)(2,1)S(1)} %copy-done, f32[256]{0:T(256)S(1)} %copy-done.18, f32[4096]{0:T(1024)S(1)} %bitcast.345, bf16[1,4096,768]{2,1,0:T(8,128)(2,1)} %all-gather.5.cloned.1.call-done, bf16[256,128]{0,1:T(8,128)(2,1)S(1)} %fusion.114, ...), kind=kOutput, calls=%fused_computation.58 | convolution fusion | flops 1619128064 | bytes 13002752 | tf_op jit(solution)/shard_map/dot_general | solution.py:97
  162.6 1.9 fusion.18
  164.6 4.3 pad_maximum_fusion
  169.6 2.1 fusion.35
  171.7 4.5 collective-permute-done
  176.2 24.0 %all_gather.21 = bf16[1,4096]{1,0:T(2,128)(2,1)S(1)} all-gather(bf16[1,512]{1,0:T(2,128)(2,1)S(1)} %collective-permute-done), channel_id=1, replica_groups=mesh['blk'=16,'fsdp'=8] {'fsdp'}, dimensions={1}, use_global_device_ids=true | all-gather | bytes 9216 | tf_op jit(solution)/shard_map/all_gather | solution.py:114
  200.3 5.8 %fusion.46 = bf16[256,4096]{1,0:T(8,128)(2,1)} fusion(bf16[256,4096]{1,0:T(8,128)(2,1)S(1)} %copy-done, bf16[256,4096]{1,0:T(8,128)(2,1)} %param.16, f32[256,4096]{1,0:T(8,128)} %get-tuple-element.16, f32[256]{0:T(256)S(1)} %broadcast_multiply_fusion, f32[256]{0:T(256)S(1)} %copy-done.19, f32[256]{0:T(256)S(1)} %copy-done.18, f32[4096]{0:T(1024)S(1)} %bitcast.347), kind=kLoop, calls=%fused_computation.62 | loop fusion | flops 9437184 | bytes 10505216 | tf_op jit(solution)/shard_map/convert_element_type | solution.py:108
  206.0 10.7 %all-gather.9.cloned.1.call-done = bf16[1,4096,768]{2,1,0:T(8,128)(2,1)} async-done(((bf16[1,512,768]{2,1,0:T(8,128)(2,1)}), bf16[1,4096,768]{2,1,0:T(8,128)(2,1)}) %all-gather.9.cloned.1.call-update) | async-done | bytes 6291472 | tf_op jit(solution)/shard_map/all_gather | solution.py:115
  216.7 5.3 fusion.104
  222.2 1.5 fusion.207
  224.5 3.2 fusion.21
  227.8 41.6 %all-gather.11.cloned.1.call-done = bf16[1,512,4096]{2,1,0:T(8,128)(2,1)} async-done(((bf16[1,512,512]{2,1,0:T(8,128)(2,1)}), bf16[1,512,4096]{2,1,0:T(8,128)(2,1)}) %all-gather.11.cloned.1.call-update) | async-done | bytes 4194320 | tf_op jit(solution)/shard_map/all_gather | solution.py:116
  269.4 3.5 fusion.110
  274.1 2.2 fusion.115
  276.3 2.9 convolution_convert_fusion.6
  279.2 1.9 fusion.116
  281.1 5.1 fusion.60
  286.2 1.9 fusion.19
  288.2 4.3 pad_maximum_fusion.1
  292.5 3.2 copy.38
  296.4 4.7 fusion.91
  302.7 3.9 fusion.32
  306.6 1.3 copy-done.3
  307.9 4.8 fusion.96
  314.0 2.7 convolution_convert_fusion.8
  316.7 6.9 %reduce-scatter.9.cloned.1.call-done = bf16[1,512,512]{2,1,0:T(8,128)(2,1)} async-done(((bf16[1,512,4096]{2,1,0:T(8,128)(2,1)}), bf16[1,512,512]{2,1,0:T(8,128)(2,1)}) %reduce-scatter.9.cloned.1.call-update) | async-done | bytes 524304 | tf_op jit(solution)/shard_map/reduce_scatter | solution.py:137
  323.5 2.0 add_convert_fusion.1
  325.5 72.6 %reduce-scatter.5.cloned.1.call-done = bf16[1,512,769]{1,2,0:T(8,128)(2,1)} async-done(((bf16[1,4096,769]{1,2,0:T(8,128)(2,1)}), bf16[1,512,769]{1,2,0:T(8,128)(2,1)}) %reduce-scatter.5.cloned.1.call-update) | async-done | bytes 787472 | tf_op jit(solution)/shard_map/reduce_scatter | solution.py:17
  398.1 1.9 add_convert_fusion
  400.1 4.9 fusion.28
  405.0 47.5 %reduce-scatter.11.cloned.1.call-done = bf16[1,512,512]{2,1,0:T(8,128)(2,1)} async-done(((bf16[1,512,4096]{2,1,0:T(8,128)(2,1)}), bf16[1,512,512]{2,1,0:T(8,128)(2,1)}) %reduce-scatter.11.cloned.1.call-update) | async-done | bytes 524304 | tf_op jit(solution)/shard_map/reduce_scatter | solution.py:137
  452.5 2.2 convert_add_fusion.3
  455.4 72.1 %reduce-scatter.7.cloned.1.call-done = bf16[1,512,769]{1,2,0:T(8,128)(2,1)} async-done(((bf16[1,4096,769]{1,2,0:T(8,128)(2,1)}), bf16[1,512,769]{1,2,0:T(8,128)(2,1)}) %reduce-scatter.7.cloned.1.call-update) | async-done | bytes 787472 | tf_op jit(solution)/shard_map/reduce_scatter | solution.py:17
  527.5 1.6 convert_add_fusion.2
  529.1 1.6 copy.43
  530.8 1.3 fusion.164
  (103 shorter events, 14.0 us)
Async XLA Ops:
  7.2 103.4 %copy-start = (bf16[256,4096]{1,0:T(8,128)(2,1)S(1)}, bf16[256,4096]{1,0:T(8,128)(2,1)}, u32[]{:S(2)}) copy-start(bf16[256,4096]{1,0:T(8,128)(2,1)} %param.14) | copy-start | bytes 6291460
  7.2 103.2 %copy-start.20 = (s32[1,256]{1,0:T(1,128)S(1)}, s32[1,256]{1,0:T(1,128)}, u32[]{:S(2)}) copy-start(s32[1,256]{1,0:T(1,128)} %param.17) | copy-start | bytes 3076
  7.2 103.4 %all-gather.5.cloned.1.call-start = ((), (), s32[]{:S(2)}) async-start(), calls=%async_computation.4 | async-start | bytes 7077888 | tf_op jit(solution)/shard_map/all_gather | solution.py:115
  7.9 135.2 %all-gather.7.cloned.1.call-start = ((), (), s32[]{:S(2)}) async-start(), calls=%async_computation.5 | async-start | bytes 4718592 | tf_op jit(solution)/shard_map/all_gather | solution.py:116
  8.7 208.0 %all-gather.9.cloned.1.call-start = ((), (), s32[]{:S(2)}) async-start(), calls=%async_computation.6 | async-start | bytes 7077888 | tf_op jit(solution)/shard_map/all_gather | solution.py:115
  8.7 15.8 %collective-permute-start.1 = (bf16[1,512,768]{2,1,0:T(8,128)(2,1)}, bf16[1,512,768]{2,1,0:T(8,128)(2,1)S(1)}, u32[]{:S(2)}, u32[]{:S(2)}) collective-permute-start(bf16[1,512,768]{2,1,0:T(8,128)(2,1)} %param.19), channel_id=1, source_target_pairs={{0,8},{8,16},{16,24},{24,32},{32,40},{40,48},{48,56},{56,64},{64,7... | collective-permute-start | bytes 2359304 | tf_op jit(solution)/shard_map/ppermute | solution.py:27
  24.5 0.9 copy-start.7
  25.4 244.0 %all-gather.11.cloned.1.call-start = ((), (), s32[]{:S(2)}) async-start(), calls=%async_computation.7 | async-start | bytes 4718592 | tf_op jit(solution)/shard_map/all_gather | solution.py:116
  25.5 18.1 %collective-permute-start.2 = (bf16[1,512,512]{2,1,0:T(8,128)(2,1)}, bf16[1,512,512]{2,1,0:T(8,128)(2,1)S(1)}, u32[]{:S(2)}, u32[]{:S(2)}) collective-permute-start(bf16[1,512,512]{2,1,0:T(8,128)(2,1)} %param.20), channel_id=1, source_target_pairs={{0,8},{8,16},{16,24},{24,32},{32,40},{40,48},{48,56},{56,64},{64,7... | collective-permute-start | bytes 1572872 | tf_op jit(solution)/shard_map/ppermute | solution.py:27
  43.6 0.8 copy-start.8
  44.4 279.1 %reduce-scatter.9.cloned.1.call-start = ((), (), s32[]{:S(2)}) async-start(), calls=%async_computation.10 | async-start | bytes 4718592 | tf_op jit(solution)/shard_map/reduce_scatter | solution.py:137
  110.4 4.9 copy-start.17
  110.5 43.0 %copy-start.15 = (pred[256,256]{0,1:T(8,128)(4,1)}, pred[256,256]{0,1:T(8,128)(4,1)S(1)}, u32[]{:S(2)}) copy-start(pred[256,256]{0,1:T(8,128)(4,1)S(1)} %fusion.141) | copy-start | bytes 196612
  115.3 2.5 copy-start.10
  115.4 7.3 %copy-start.14 = (bf16[256,512]{0,1:T(8,128)(2,1)}, bf16[256,512]{0,1:T(8,128)(2,1)S(1)}, u32[]{:S(2)}) copy-start(bf16[256,512]{0,1:T(8,128)(2,1)S(1)} %copy.66) | copy-start | bytes 786436
  117.0 5.7 %copy-start.25 = (f32[4,256]{1,0:T(4,128)}, f32[4,256]{1,0:T(4,128)S(1)}, u32[]{:S(2)}) copy-start(f32[4,256]{1,0:T(4,128)S(1)} %get-tuple-element.14) | copy-start | bytes 12292
  122.7 275.4 %reduce-scatter.5.cloned.1.call-start = ((), (), s32[]{:S(2)}) async-start(), calls=%async_computation.8 | async-start | bytes 7151616 | tf_op jit(solution)/shard_map/reduce_scatter | solution.py:17
  153.5 1.8 copy-start.11
  153.5 1.8 copy-start.18
  168.9 0.7 copy-start.22
  168.9 31.3 %copy-start.19 = (f32[256]{0:T(256)S(1)}, f32[256]{0:T(256)}, u32[]{:S(2)}) copy-start(f32[256]{0:T(256)} %get-tuple-element.10) | copy-start | bytes 3076
  168.9 283.6 %reduce-scatter.11.cloned.1.call-start = ((), (), s32[]{:S(2)}) async-start(), calls=%async_computation.11 | async-start | bytes 4718592 | tf_op jit(solution)/shard_map/reduce_scatter | solution.py:137
  169.6 6.6 %collective-permute-start = (bf16[1,512]{1,0:T(2,128)(2,1)S(1)}, bf16[1,512]{1,0:T(2,128)(2,1)S(1)}, u32[]{:S(2)}, u32[]{:S(2)}) collective-permute-start(bf16[1,512]{1,0:T(2,128)(2,1)S(1)} %copy-done.22), channel_id=1, source_target_pairs={{0,8},{8,16},{16,24},{24,32},{32,40},{40,48},{48,56},{56,64},{64,7... | collective-permute-start | bytes 3080 | tf_op jit(solution)/shard_map/ppermute | solution.py:27
  216.7 5.5 %copy-start.16 = (pred[256,256]{0,1:T(8,128)(4,1)S(1)}, pred[256,256]{0,1:T(8,128)(4,1)}, u32[]{:S(2)}) copy-start(pred[256,256]{0,1:T(8,128)(4,1)} %copy-done.15) | copy-start | bytes 196612
  222.0 2.5 copy-start.9
  222.0 2.5 copy-start.5
  222.2 5.6 %copy-start.13 = (bf16[256,512]{0,1:T(8,128)(2,1)}, bf16[256,512]{0,1:T(8,128)(2,1)S(1)}, u32[]{:S(2)}) copy-start(bf16[256,512]{0,1:T(8,128)(2,1)S(1)} %copy.68) | copy-start | bytes 786436
  227.7 299.8 %reduce-scatter.7.cloned.1.call-start = ((), (), s32[]{:S(2)}) async-start(), calls=%async_computation.9 | async-start | bytes 7151616 | tf_op jit(solution)/shard_map/reduce_scatter | solution.py:17
  276.3 4.8 copy-start.1
  279.2 1.9 copy-start.12
  292.5 3.2 copy-start.2
  292.5 3.7 copy-start.21
  306.6 1.3 copy-start.3
  312.7 0.7 copy-start.24
  313.4 10.1 %copy-start.6 = (f32[1,512,512]{2,1,0:T(8,128)S(1)}, f32[1,512,512]{2,1,0:T(8,128)}, u32[]{:S(2)}) copy-start(f32[1,512,512]{2,1,0:T(8,128)} %param.23) | copy-start | bytes 3145732
  314.0 86.1 %copy-start.4 = (bf16[256,4096]{1,0:T(8,128)(2,1)S(1)}, bf16[256,4096]{1,0:T(8,128)(2,1)}, u32[]{:S(2)}) copy-start(bf16[256,4096]{1,0:T(8,128)(2,1)} %copy-done.3) | copy-start | bytes 6291460
  325.5 79.5 %collective-permute-start.5 = (bf16[1,512,512]{2,1,0:T(8,128)(2,1)}, bf16[1,512,512]{2,1,0:T(8,128)(2,1)S(1)}, u32[]{:S(2)}, u32[]{:S(2)}) collective-permute-start(bf16[1,512,512]{2,1,0:T(8,128)(2,1)} %add_convert_fusion.1), channel_id=1, source_target_pairs={{0,8},{8,16},{16,24},{24,32},{32,40},{40,48},{48,56},{56,64},{64,7... | collective-permute-start | bytes 1572872 | tf_op jit(solution)/shard_map/ppermute | solution.py:27
  400.0 127.5 %collective-permute-start.4 = (bf16[1,512,768]{1,2,0:T(8,128)(2,1)S(1)}, bf16[1,512,768]{1,2,0:T(8,128)(2,1)}, u32[]{:S(2)}, u32[]{:S(2)}) collective-permute-start(bf16[1,512,768]{1,2,0:T(8,128)(2,1)S(1)} %add_convert_fusion), channel_id=1, source_target_pairs={{0,8},{8,16},{16,24},{24,32},{32,40},{40,48},{48,56},{56,64},{64,7... | collective-permute-start | bytes 2359304 | tf_op jit(solution)/shard_map/ppermute | solution.py:27
  400.1 54.6 %copy-start.23 = (f32[1,512]{1,0:T(1,128)S(1)}, f32[1,512]{1,0:T(1,128)}, u32[]{:S(2)}) copy-start(f32[1,512]{1,0:T(1,128)} %param.21) | copy-start | bytes 6148
  455.4 75.4 %collective-permute-start.3 = (bf16[1,512]{1,0:T(2,128)(2,1)S(1)}, bf16[1,512]{1,0:T(2,128)(2,1)S(1)}, u32[]{:S(2)}, u32[]{:S(2)}) collective-permute-start(bf16[1,512]{1,0:T(2,128)(2,1)S(1)} %fusion.167), channel_id=1, source_target_pairs={{0,8},{8,16},{16,24},{24,32},{32,40},{40,48},{48,56},{56,64},{64,7... | collective-permute-start | bytes 3080 | tf_op jit(solution)/shard_map/ppermute | solution.py:27
Sparse Core Ops, SparseCore 0:
  9.7 74.8 all-gather.4
  86.2 56.8 all-gather.6
  145.4 71.2 all-gather.8
  218.2 51.1 all-gather.10
  271.6 51.8 reduce-scatter.8
  325.8 72.2 reduce-scatter.4
  400.5 51.9 reduce-scatter.10
  454.9 72.4 reduce-scatter.6
where the time goes:
time: 545 us; the launch traced here: 539 us
  waiting for transfers between devices  311 us (57%)
  blocking collectives  87.2 us (16%)
  matrix products  85.6 us (16%)
  other arithmetic  29.6 us (5%)
  between operations  15 us (3%)
  local copies, waits for them, and re-layouts  9.84 us (2%)
    reduce_scatter x2, waiting for transfers between devices, sent_together(): result = lax.psum_scatter(both, axis, scatter_dimension=dim, tiled=True)  145 us
    all_gather x2, blocking collectives, gather_layer(): lax.all_gather(gain_piece, 'fsdp', axis=1, tiled=True)  87.2 us
    all_gather x2, waiting for transfers between devices, gather_layer(): lax.all_gather(proj_piece, 'fsdp', axis=2, tiled=True)  61.8 us
    reduce_scatter x2, waiting for transfers between devices, reduce_terms(): lax.psum_scatter(grad_terms[2][None].astype(jnp.bfloat16), 'fsdp', scatte...  54.4 us
    ppermute x6, waiting for transfers between devices, shifted(): return lax.ppermute(value, axis, pairs)  38.3 us
    dot_general x4, matrix products, layer_parts(): jnp.dot(normed, qkv_weight, preferred_element_type=jnp.float32)  19.4 us
    dot_general x2, matrix products, layer_backward(): lax.dot_general(d_projected, qkv_weight, (((1,), (1,)), ((), ())), prefer...  12.4 us
  transfers between devices with their start and end apart: 14, of which 10 were waited for; matrix products, arithmetic and copies ran while one was open for 22% of the time, Pallas kernels for 0%

commit v1 on v0

v1 whole, which is shorter than its diff:
```python
import functools

import jax
import jax.numpy as jnp
from jax import lax
from jax.experimental import pallas as pl
from jax.experimental.pallas import tpu as pltpu
from jax.sharding import PartitionSpec as P

HEADS = 4
PAD = 16
VMEM_LIMIT = 64 * 1024 * 1024 - 256 * 1024
MESH = pl.DeviceIdType.MESH
F32, BF16 = jnp.float32, jnp.bfloat16

MESSAGES = (
    "xe", "seg", "pR", "pL", "qZ", "qR", "qL", "pZ0", "pZ1", "pZ2", "pZ3", "pRf", "pLf", "cR", "cL",
    "eR", "eL", "dh0", "dh1", "dh2", "dh3", "hid", "res", "m1R", "m1L", "m2R", "m2L", "m3R", "m3L",
    "mZ0", "mZ1", "z0", "z1", "z2", "z3", "p1R", "p1L", "p2R", "p2L", "p3R", "p3L", "fq0", "fq1", "fp",
)
LOADS = (
    "wq", "wg", "wp", "xs", "xf", "cot", "sf", "sb", "sg", "sq", "sp", "oq0", "oq1", "op", "og",
)


def dot(a, b):
    return lax.dot_general(a, b, (((1,), (0,)), ((), ())), preferred_element_type=F32)


def dot_nt(a, b):
    return lax.dot_general(a, b, (((1,), (1,)), ((), ())), preferred_element_type=F32)


def dot_tn(a, b):
    return lax.dot_general(a, b, (((0,), (0,)), ((), ())), preferred_element_type=F32)


def kernel(
    n_blk, xf_in, xs_in, xe_in, cot_in, sf_in, sb_in, qkv_in, gain_in, proj_in, sg_in, sq_in, sp_in,
    out_h, out_g, out_q, out_p,
    Wq, Wp, Gq, Gp, RQ, RPZ, RPX, X, XE, COT, HID, DH, DN, NS, ACC, PR, ATTN, ATT_T, PROBS, DP, DATT, DACC,
    MASK, GK, GV, INV, CO, GG, SEGI, SEG, GN, SG, SQ, SP, FQ, FP, go, send_sem, recv_sem, load_sem,
):
    T, D = COT.shape
    C = Wq.shape[1] - PAD
    Q = Wq.shape[2]
    A = Wp.shape[1]
    HD = A // HEADS
    H2 = A // 2
    scale = HD ** (-0.5)

    b, f = lax.axis_index("blk"), lax.axis_index("fsdp")
    z, x = lax.div(f, 4), lax.rem(f, 4)
    odd = lax.rem(b, 2)

    def at(zz, xx):
        return lax.rem(zz, 2) * 4 + lax.rem(xx, 4)

    own, jL, jR, jF = f, at(z, x + 3), at(z, x + 1), at(z, x + 2)
    oz, ozL, ozR, ozF = at(z + 1, x), at(z + 1, x + 3), at(z + 1, x + 1), at(z + 1, x + 2)
    right, left, across = (b, jR), (b, jL), (b, oz)
    prev = (lax.rem(b + n_blk - 1, n_blk), lax.rem(f + 4 * (1 - odd), 8))
    following = (lax.rem(b + 1, n_blk), lax.rem(f + 4 * odd, 8))
    z_keep, z_send = z + odd, z + 1 + odd

    started = []

    def remote(name, src, dst, device):
        k = MESSAGES.index(name)
        return pltpu.make_async_remote_copy(
            src_ref=src, dst_ref=dst, send_sem=send_sem.at[k], recv_sem=recv_sem.at[k],
            device_id=device, device_id_type=MESH,
        )

    def send(name, src, dst, device):
        copy = remote(name, src, dst, device)
        copy.start()
        started.append(copy)

    def arrived(name, dst):
        remote(name, dst, dst, right).wait_recv()

    loads = {}

    def load(name, src, dst):
        loads[name] = pltpu.make_async_copy(src, dst, load_sem.at[LOADS.index(name)])
        loads[name].start()

    def cols(j):
        return pl.ds(pl.multiple_of(j * C, C), C)

    def wide(v):
        return jnp.concatenate([v] * (C // v.shape[1]), axis=1) if C > v.shape[1] else v

    def folded(v):
        total = v[:, 0:128]
        for k in range(1, v.shape[1] // 128):
            total = total + v[:, k * 128 : (k + 1) * 128]
        return total

    load("wp", proj_in, Wp.at[own])
    load("wq", qkv_in, Wq.at[own, pl.ds(0, C)])
    load("wg", gain_in, GN)
    load("sf", sf_in, SEGI.at[0])
    load("sb", sb_in, SEGI.at[1])
    load("xs", xs_in, X.at[0])
    load("xf", xf_in, X.at[1])
    load("cot", cot_in, COT)
    load("sg", sg_in, SG)
    load("sq", sq_in, SQ)
    load("sp", sp_in, SP)
    barrier = pltpu.get_barrier_semaphore()
    for device in (right, left, across, prev, following):
        pl.semaphore_signal(barrier, inc=1, device_id=device, device_id_type=MESH)
    loads["wg"].wait()
    loads["sf"].wait()
    loads["sb"].wait()
    loads["wp"].wait()
    loads["wq"].wait()
    Wq[own, C : C + PAD, 0:C] = jnp.broadcast_to(GN[...].astype(F32), (PAD, C)).astype(BF16)
    Wq[own, C : C + PAD, C:Q] = jnp.zeros((PAD, Q - C), BF16)
    SEG[0, 0] = jnp.broadcast_to(SEGI[0].astype(F32), (8, T))
    SEG[0, 1] = jnp.broadcast_to(SEGI[1].astype(F32), (8, T))
    pl.semaphore_wait(barrier, 5)

    send("xe", xe_in, XE, prev)
    send("seg", SEG.at[0], SEG.at[1], prev)

    @pl.when(odd == 1)
    def _():
        pl.semaphore_wait(go, 1)

    send("pR", Wp.at[own], Wp.at[own], right)
    send("pL", Wp.at[own], Wp.at[own], left)
    send("qZ", Wq.at[own], Wq.at[own], across)
    send("qR", Wq.at[own], Wq.at[own], right)
    send("qL", Wq.at[own], Wq.at[own], left)
    send("pZ0", Wp.at[own], Wp.at[own], across)

    def make_mask(place, kind, slot):
        row = jnp.broadcast_to(SEG[place, kind, 0:1, :], (T, T))
        col = row.T
        i = lax.broadcasted_iota(jnp.int32, (T, T), 0)
        j = lax.broadcasted_iota(jnp.int32, (T, T), 1)
        MASK[slot] = jnp.where((j <= i) & (row == col), 1.0, 0.0)

    def rms(read, slot):
        def step(j, total):
            v = read(cols(j)).astype(F32)
            return total + folded(v * v)

        total = lax.fori_loop(0, 8, step, jnp.zeros((T, 128), F32))
        inv = lax.rsqrt(jnp.sum(total, axis=1, keepdims=True) * (1.0 / D) + 1e-05)
        INV[slot] = jnp.broadcast_to(inv, (T, 128))

    def gain_row(j):
        return Wq[j, C : C + PAD, 0:C][0:1, :].astype(F32)

    def normed(read, slot, j):
        v = read(cols(j)).astype(F32)
        return (v * wide(INV[slot]) * gain_row(j)).astype(BF16)

    def read_s(c):
        return X[0, :, c]

    def read_f(c):
        return X[1, :, c]

    def read_e(c):
        return XE[:, c]

    def read_h(c):
        return HID[:, c]

    def project_piece(j):
        for i, read in ((0, read_s), (1, read_f), (2, read_e)):
            block = normed(read, i, j)
            if i == 0:
                NS[j] = block
            ACC[i] += dot(block, Wq[j, 0:C, :])

    def project_all(read, slot, dst):
        rms(read, slot)
        ACC[0] = jnp.zeros((T, Q), F32)

        def step(j, carry):
            ACC[0] += dot(normed(read, slot, j), Wq[j, 0:C, :])
            return carry

        lax.fori_loop(0, 8, step, 0)
        PR[dst] = ACC[0].astype(BF16)

    def head(h):
        return slice(h * HD, (h + 1) * HD)

    def attention(src, mask_slot, probs, t_off):
        def step(h, carry):
            allowed = MASK[mask_slot] > 0.5
            s = dot_nt(PR[src, :, head(h)], PR[src, :, A : A + HD]) * scale
            s = jnp.where(allowed, s, -1e30)
            e = jnp.where(allowed, jnp.exp(s - jnp.max(s, axis=1, keepdims=True)), 0.0)
            p = e / jnp.sum(e, axis=1, keepdims=True)
            if probs:
                PROBS[h] = p
            out = dot(p.astype(BF16), PR[src, :, A + HD : A + 2 * HD])
            if probs:
                ATT_T[head(h), t_off : t_off + T] = out.T.astype(BF16)
            else:
                ATTN[:, head(h)] = out.astype(BF16)
            return carry

        for h in range(HEADS):
            step(h, 0)

    def attention_back(src, dst):
        GK[...] = jnp.zeros_like(GK)
        GV[...] = jnp.zeros_like(GV)

        def step(h, carry):
            d_head = DATT[:, head(h)]
            p = PROBS[h]
            dp = dot_nt(d_head, PR[src, :, A + HD : A + 2 * HD])
            inner = jnp.sum(dp * p, axis=1, keepdims=True)
            ds = (p * (dp - inner) * scale).astype(BF16)
            DP[dst, :, head(h)] = dot(ds, PR[src, :, A : A + HD]).astype(BF16)
            GK[...] += dot_tn(ds, PR[src, :, head(h)])
            GV[...] += dot_tn(p.astype(BF16), d_head)
            return carry

        for h in range(HEADS):
            step(h, 0)
        DP[dst, :, A : A + HD] = GK[...].astype(BF16)
        DP[dst, :, A + HD : A + 2 * HD] = GV[...].astype(BF16)

    def d_att_piece(j):
        DACC[...] += dot_nt(COT[:, cols(j)], Wp[j])

    make_mask(0, 1, 0)
    make_mask(0, 0, 1)
    for j in range(8):
        Gq[j, C : C + PAD, :] = jnp.zeros((PAD, Q), BF16)
    ACC[...] = jnp.zeros_like(ACC)
    DACC[...] = jnp.zeros_like(DACC)
    loads["xs"].wait()
    rms(read_s, 0)
    loads["xf"].wait()
    rms(read_f, 1)
    loads["cot"].wait()
    arrived("seg", SEG.at[1])
    make_mask(1, 1, 2)
    make_mask(1, 0, 3)

    arrived("pR", Wp.at[jL])
    send("pRf", Wp.at[jL, pl.ds(0, H2)], Wp.at[jL, pl.ds(0, H2)], right)
    send("pZ1", Wp.at[jL], Wp.at[jL], across)
    arrived("pL", Wp.at[jR])
    send("pLf", Wp.at[jR, pl.ds(H2, H2)], Wp.at[jR, pl.ds(H2, H2)], left)
    send("pZ2", Wp.at[jR], Wp.at[jR], across)
    arrived("qZ", Wq.at[oz])
    send("cR", Wq.at[oz], Wq.at[oz], right)
    send("cL", Wq.at[oz], Wq.at[oz], left)
    arrived("xe", XE)
    rms(read_e, 2)
    project_piece(own)
    arrived("pRf", Wp.at[jF, pl.ds(0, H2)])
    arrived("pLf", Wp.at[jF, pl.ds(H2, H2)])
    send("pZ3", Wp.at[jF], Wp.at[jF], across)
    arrived("qR", Wq.at[jL])
    send("eR", Wq.at[jL], Wq.at[jL], right)
    project_piece(oz)
    project_piece(jL)
    arrived("qL", Wq.at[jR])
    project_piece(jR)
    d_att_piece(own)
    d_att_piece(jL)
    d_att_piece(jR)
    d_att_piece(jF)
    arrived("cL", Wq.at[ozR])
    send("eL", Wq.at[ozR], Wq.at[ozR], left)

    @pl.when(odd == 0)
    def _():
        pl.semaphore_signal(go, inc=1, device_id=following, device_id_type=MESH)

    project_piece(ozR)
    arrived("cR", Wq.at[ozL])
    project_piece(ozL)
    arrived("pZ0", Wp.at[oz])
    d_att_piece(oz)
    arrived("pZ1", Wp.at[ozL])
    d_att_piece(ozL)
    arrived("pZ2", Wp.at[ozR])
    d_att_piece(ozR)
    arrived("eR", Wq.at[jF])
    project_piece(jF)
    arrived("eL", Wq.at[ozF])
    project_piece(ozF)
    PR[0] = ACC[0].astype(BF16)
    PR[1] = ACC[1].astype(BF16)
    PR[2] = ACC[2].astype(BF16)
    attention(0, 0, True, 0)
    arrived("pZ3", Wp.at[ozF])
    d_att_piece(ozF)
    DATT[...] = DACC[...].astype(BF16)

    attention_back(0, 0)

    def scaled_piece(j, total):
        d_normed = dot_nt(DP[0], Wq[j, 0:C, :])
        v = X[0, :, cols(j)].astype(F32)
        GG[j] = jnp.broadcast_to(jnp.sum(d_normed * (v * wide(INV[0])), axis=0, keepdims=True), (8, C))
        scaled = d_normed * gain_row(j)
        DN[j] = scaled
        return total + folded(scaled * v)

    total = lax.fori_loop(0, 8, scaled_piece, jnp.zeros((T, 128), F32))
    inv = INV[0]
    CO[...] = inv * inv * inv * (jnp.sum(total, axis=1, keepdims=True) * (1.0 / D))
    for k in range(4):
        rows = slice(k * (T // 4), (k + 1) * (T // 4))

        def dx_piece(j, carry):
            v = X[0, rows, cols(j)].astype(F32)
            d_wide = wide(INV[0, rows, :]) * DN[j, rows, :] - v * wide(CO[rows, :])
            X[0, rows, cols(j)] = (COT[rows, cols(j)].astype(F32) + d_wide).astype(BF16)
            return carry

        lax.fori_loop(0, 8, dx_piece, 0)
        send(f"dh{k}", X.at[0, pl.ds(k * (T // 4), T // 4)], DH.at[pl.ds(k * (T // 4), T // 4)], prev)

    hidden_copy = remote("hid", X.at[1], HID, prev)
    started.append(hidden_copy)

    def forward_one():
        attention(1, 1, False, 0)

        def out_piece(j, carry):
            X[1, :, cols(j)] = (X[1, :, cols(j)].astype(F32) + dot(ATTN[...], Wp[j])).astype(BF16)
            return carry

        lax.fori_loop(0, 8, out_piece, 0)
        hidden_copy.start()

    attention(2, 2, True, T)
    pl.when(odd == 0)(forward_one)
    loads["sg"].wait()
    loads["sq"].wait()
    loads["sp"].wait()

    for k in range(4):
        arrived(f"dh{k}", DH.at[pl.ds(k * (T // 4), T // 4)])

    DACC[...] = jnp.zeros_like(DACC)

    def d_att_two(j, carry):
        DACC[...] += dot_nt(DH[:, cols(j)], Wp[j])
        return carry

    lax.fori_loop(0, 8, d_att_two, 0)
    DATT[...] = DACC[...].astype(BF16)
    attention_back(2, 1)

    def is_own(j):
        return jnp.where(j == own, 1.0, 0.0)

    def grad_qkv(j):
        d_normed = dot_nt(DP[1], Wq[j, 0:C, :])
        xi = XE[:, cols(j)].astype(F32) * wide(INV[2])
        gg = GG[j][0:1, :] + jnp.sum(d_normed * xi, axis=0, keepdims=True)
        Gq[j, C : C + PAD, 0:C] = (jnp.broadcast_to(gg, (PAD, C)) + is_own(j) * SG[...]).astype(BF16)
        block = (xi * gain_row(j)).astype(BF16)
        terms = dot_tn(NS[j], DP[0]) + dot_tn(block, DP[1])
        Gq[j, 0:C, :] = (terms + is_own(j) * SQ[...]).astype(BF16)

    def grad_proj(j):
        terms = dot(ATT_T[:, 0:T], COT[:, cols(j)]) + dot(ATT_T[:, T : 2 * T], DH[:, cols(j)])
        Gp[j] = (terms + is_own(j) * SP[...]).astype(BF16)

    def each(count, work):
        def step(k, carry):
            work(k)
            return carry

        lax.fori_loop(0, count, step, 0)

    QR = 48 if (C + PAD) % 48 == 0 else 16

    def add_q(j, slots, first=0, last=C + PAD):
        def work(k):
            rows = pl.ds(pl.multiple_of(first + k * QR, 16), QR)
            v = Gq[j, rows, :].astype(F32)
            for s in slots:
                v = v + RQ[s, rows, :].astype(F32)
            Gq[j, rows, :] = v.astype(BF16)

        each((last - first) // QR, work)

    def add_p(j, base, size, parts):
        def work(k):
            off = pl.multiple_of(k * 16, 16)
            v = Gp[j, pl.ds(base + off, 16), :].astype(F32)
            for ref in parts:
                v = v + ref[pl.ds(off, 16), :].astype(F32)
            Gp[j, pl.ds(base + off, 16), :] = v.astype(BF16)

        each(size // 16, work)

    each(2, lambda k: grad_qkv(at(z + k, x + 2)))
    send("m1R", Gq.at[jF], RQ.at[0], right)
    send("m1L", Gq.at[ozF], RQ.at[1], left)
    each(4, lambda k: grad_proj(at(z_send, k)))
    for q, off in enumerate((2, 1, 3, 0)):
        send(f"z{q}", Gp.at[at(z_send, x + off)], RPZ.at[q], across)
    each(2, lambda k: grad_qkv(at(z + 1 + k, x + 1 + 2 * k)))
    send("m2R", Gq.at[ozR], RQ.at[2], right)
    send("m2L", Gq.at[jL], RQ.at[3], left)
    pl.when(odd == 1)(forward_one)
    each(2, lambda k: grad_qkv(at(z + k, x + 1 + 2 * k)))
    each(2, lambda k: grad_qkv(at(z + k, x)))
    each(4, lambda k: grad_proj(at(z_keep, k)))
    arrived("m1R", RQ.at[0])
    add_q(jR, (0,))
    send("m3R", Gq.at[jR], RQ.at[4], right)
    arrived("m1L", RQ.at[1])
    add_q(ozL, (1,))
    send("m3L", Gq.at[ozL], RQ.at[5], left)

    arrived("hid", HID)
    project_all(read_h, 3, 1)
    attention(1, 3, False, 0)

    def result_piece(j, carry):
        HID[:, cols(j)] = (HID[:, cols(j)].astype(F32) + dot(ATTN[...], Wp[j])).astype(BF16)
        return carry

    lax.fori_loop(0, 8, result_piece, 0)
    send("res", HID, out_h, following)

    kF, kR, kL, kO = (at(z_keep, x + off) for off in (2, 1, 3, 0))
    top, low = pl.ds(0, H2), pl.ds(H2, H2)
    arrived("z0", RPZ.at[0])
    add_p(kF, 0, A, (RPZ.at[0],))
    send("p1R", Gp.at[kF, top], RPX.at[0], right)
    send("p1L", Gp.at[kF, low], RPX.at[1], left)
    arrived("z1", RPZ.at[1])
    add_p(kR, 0, A, (RPZ.at[1],))
    send("p2R", Gp.at[kR, low], RPX.at[2], right)
    arrived("z2", RPZ.at[2])
    add_p(kL, 0, A, (RPZ.at[2],))
    send("p2L", Gp.at[kL, top], RPX.at[3], left)
    arrived("m2R", RQ.at[2])
    arrived("m2L", RQ.at[3])
    arrived("m3R", RQ.at[4])
    arrived("m3L", RQ.at[5])
    j_send, j_keep = at(z_send, x), at(z_keep, x)
    cut = (C + PAD) // QR // 2 * QR
    part0, part1 = pl.ds(0, cut), pl.ds(cut, C + PAD - cut)
    add_q(j_send, (2 + odd, 5 - odd))
    send("mZ0", Gq.at[j_send, part0], RQ.at[6, part0], across)
    send("mZ1", Gq.at[j_send, part1], RQ.at[6, part1], across)
    arrived("p1R", RPX.at[0])
    add_p(kR, 0, H2, (RPX.at[0],))
    send("p3R", Gp.at[kR, top], RPX.at[4], right)
    arrived("p1L", RPX.at[1])
    add_p(kL, H2, H2, (RPX.at[1],))
    send("p3L", Gp.at[kL, low], RPX.at[5], left)
    add_q(j_keep, (3 - odd, 4 + odd))
    arrived("z3", RPZ.at[3])
    arrived("p2R", RPX.at[2])
    arrived("p2L", RPX.at[3])
    arrived("p3R", RPX.at[4])
    arrived("p3L", RPX.at[5])
    add_p(kO, 0, H2, (RPZ.at[3, top], RPX.at[4], RPX.at[3]))
    add_p(kO, H2, H2, (RPZ.at[3, low], RPX.at[2], RPX.at[5]))
    send("fp", Gp.at[kO], FP, following)
    arrived("mZ0", RQ.at[6, part0])
    add_q(j_keep, (6,), 0, cut)
    send("fq0", Gq.at[j_keep, part0], FQ.at[part0], following)
    arrived("mZ1", RQ.at[6, part1])
    add_q(j_keep, (6,), cut)
    send("fq1", Gq.at[j_keep, part1], FQ.at[part1], following)

    arrived("fp", FP)
    SP[...] = FP[...].astype(F32)
    load("op", SP, out_p)
    arrived("fq0", FQ.at[part0])
    SQ[0:cut, :] = FQ[0:cut, :].astype(F32)
    load("oq0", SQ.at[part0], out_q.at[part0])
    arrived("fq1", FQ.at[part1])
    SG[...] = FQ[C : C + PAD, 0:C].astype(F32)[0:1, :]
    load("og", SG, out_g)
    SQ[cut:C, :] = FQ[cut:C, :].astype(F32)
    load("oq1", SQ.at[pl.ds(cut, C - cut)], out_q.at[pl.ds(cut, C - cut)])
    arrived("res", out_h)
    for name in ("op", "oq0", "og", "oq1"):
        loads[name].wait()
    for copy in started:
        copy.wait_send()


def body(
    n_blk, x_forward, seg_forward, x_saved, x_earlier, cotangent, seg_backward,
    gain, qkv, proj, sum_gain, sum_qkv, sum_proj,
):
    T, D = x_forward.shape
    C, Q = qkv.shape[1:]
    A = proj.shape[1]
    HD = A // HEADS
    anywhere = pl.BlockSpec(memory_space=pl.ANY)
    V = pltpu.VMEM
    scratch = [
        V((8, C + PAD, Q), BF16), V((8, A, C), BF16), V((8, C + PAD, Q), BF16), V((8, A, C), BF16),
        V((7, C + PAD, Q), BF16), V((4, A, C), BF16), V((6, A // 2, C), BF16),
        V((2, T, D), BF16), V((T, D), BF16), V((T, D), BF16), V((T, D), BF16), V((T, D), BF16),
        V((8, T, C), F32), V((8, T, C), BF16), V((3, T, Q), F32), V((3, T, Q), BF16),
        V((T, A), BF16), V((A, 2 * T), BF16), V((HEADS, T, T), F32), V((2, T, Q), BF16),
        V((T, A), BF16), V((T, A), F32), V((4, T, T), F32), V((T, HD), F32), V((T, HD), F32),
        V((4, T, 128), F32), V((T, 128), F32), V((8, 8, C), F32), V((2, 1, T), jnp.int32),
        V((2, 2, 8, T), F32), V((1, C), BF16), V((1, C), F32), V((C, Q), F32), V((A, C), F32),
        V((C + PAD, Q), BF16), V((A, C), BF16), pltpu.SemaphoreType.REGULAR,
        pltpu.SemaphoreType.DMA((len(MESSAGES),)),
        pltpu.SemaphoreType.DMA((len(MESSAGES),)),
        pltpu.SemaphoreType.DMA((len(LOADS),)),
    ]
    hidden, new_g, new_q, new_p = pl.pallas_call(
        functools.partial(kernel, n_blk),
        out_shape=(
            jax.ShapeDtypeStruct((T, D), BF16),
            jax.ShapeDtypeStruct((1, C), F32),
            jax.ShapeDtypeStruct((C, Q), F32),
            jax.ShapeDtypeStruct((A, C), F32),
        ),
        in_specs=[anywhere] * 12,
        out_specs=(anywhere,) * 4,
        scratch_shapes=scratch,
        compiler_params=pltpu.CompilerParams(
            collective_id=0, has_side_effects=True, vmem_limit_bytes=VMEM_LIMIT
        ),
        name="two_steps",
    )(
        x_forward, x_saved, x_earlier, cotangent, seg_forward, seg_backward, qkv[0], gain, proj[0],
        sum_gain, sum_qkv[0], sum_proj[0],
    )
    return hidden, new_g, new_q[None], new_p[None]


def solution(mesh):
    rows, layer = P(("blk", "fsdp"), None), P("blk", "fsdp")
    q_spec, p_spec = P("blk", "fsdp", None), P("blk", None, "fsdp")
    return jax.shard_map(
        functools.partial(body, mesh.shape["blk"]),
        mesh=mesh,
        in_specs=(rows,) * 6 + (layer, q_spec, p_spec) * 2,
        out_specs=(rows, layer, q_spec, p_spec),
        check_vma=False,
    )
```

time: 545 us -> 195 us (0.36); the launches traced: 539 us -> 195 us
  waiting for transfers between devices: 311 us -> 0 us
  Pallas kernels: 0 us -> 188 us
  blocking collectives: 87.2 us -> 0 us
  matrix products: 85.6 us -> 0 us
  other arithmetic: 29.6 us -> 0 us
  between operations: 15 us -> 0.66 us
    reduce_scatter x4 -> x0, waiting for transfers between devices: 199 us -> none  [the longest x2 145 us: sent_together(): result = lax.psum_scatter(both, axis, scatter_dimension=dim, tiled=True)]
    pallas_call x0 -> x1, Pallas kernels: none -> 188 us  [body(): pl.pallas_call(functools.partial(kernel, n_blk), out_shape=(jax.ShapeDtyp...]
    all_gather x2 -> x0, blocking collectives: 87.2 us -> none  [gather_layer(): lax.all_gather(gain_piece, 'fsdp', axis=1, tiled=True)]
    dot_general x26 -> x0, matrix products: 81.4 us -> none  [the longest x4 19.4 us: layer_parts(): jnp.dot(normed, qkv_weight, preferred_element_type=jnp.float32)]
    all_gather x4 -> x0, waiting for transfers between devices: 72.5 us -> none  [the longest x2 61.8 us: gather_layer(): lax.all_gather(proj_piece, 'fsdp', axis=2, tiled=True)]
    ppermute x6 -> x0, waiting for transfers between devices: 38.3 us -> none  [shifted(): return lax.ppermute(value, axis, pairs)]
    convert_element_type x4 -> x0, other arithmetic: 10.3 us -> none  [the longest x1 5.77 us: layer_backward(): d_tokens = (upstream.astype(jnp.float32) + d_wide).astype(jnp.bfloat16)]
    concatenate x2 -> x0, other arithmetic: 8.65 us -> none  [sent_together(): jnp.concatenate([a.reshape(*a.shape[:along], w) for a, w in zip(arrays, w...]
  transfers between devices with their start and end apart: 14 -> 0, of which waited for: 10 -> 0; matrix products, arithmetic and copies ran while one was open for 22% -> 0% of each run, Pallas kernels for 0% -> 0%
where the time goes in v1:
time: 195 us
  Pallas kernels  188 us (96%)
  local copies, waits for them, and re-layouts  5.95 us (3%)
    pallas_call x1, Pallas kernels, body(): pl.pallas_call(functools.partial(kernel, n_blk), out_shape=(jax.ShapeDtyp...  188 us
    unnamed x10, local copies, waits for them, and re-layouts  5.95 us

profile of v1, /device:TPU:0, one launch (start us, length us, event | category | flops | bytes accessed | tf_op | source)
XLA Modules:
  0.0 195.0 jit_solution(13051864306569395828)
XLA Ops:
  0.6 188.4 %two_steps.1 = (bf16[256,4096]{1,0:T(8,128)(2,1)}, f32[1,512]{1,0:T(1,128)}, f32[512,768]{1,0:T(8,128)}, f32[512,512]{1,0:T(8,128)}) custom-call(bf16[256,4096]{1,0:T(8,128)(2,1)} %xf_in.1, bf16[256,4096]{1,0:T(8,128)(2,1)} %xs_in.1, bf16[256,4096]{1,0:T(8,128)(2,1)} %xe_in.1, bf16[256,4096]{1,0:T(8,128)(2,1)} %cot_in.1, s32[1,256]{1,0:T(1,128)} %sf_in.1, ...), custom_call_target="tpu_custom_call" | custom-call | tf_op jit(solution)/shard_map/two_steps/pallas_call | solution.py:525
  189.0 0.0 copy-start.2
  189.0 0.0 copy-start
  189.1 3.2 %copy.20 = bf16[256,4096]{1,0:T(8,128)(2,1)} copy(bf16[256,4096]{1,0:T(8,128)(2,1)} %get-tuple-element.16) | data formatting | bytes 4194304
  192.3 0.0 copy-done.2
  192.3 0.0 copy-start.1
  192.3 0.6 copy.21
  192.9 0.0 copy-done
  192.9 1.1 copy.22
  194.0 0.0 copy-done.1
  194.0 1.0 copy.23
Async XLA Ops:
  189.0 3.3 %copy-start.2 = (f32[1,512]{1,0:T(1,128)S(1)}, f32[1,512]{1,0:T(1,128)}, u32[]{:S(2)}) copy-start(f32[1,512]{1,0:T(1,128)} %get-tuple-element.17) | copy-start | bytes 6148
  189.0 3.8 %copy-start = (f32[512,768]{1,0:T(8,128)S(1)}, f32[512,768]{1,0:T(8,128)}, u32[]{:S(2)}) copy-start(f32[512,768]{1,0:T(8,128)} %get-tuple-element.10) | copy-start | bytes 4718596
  192.3 1.7 copy-start.1

commit v2 on v1

--- a/solution.py
+++ b/solution.py
@@ -14,12 +14,14 @@
 F32, BF16 = jnp.float32, jnp.bfloat16
 
 MESSAGES = (
-    "xe", "seg", "pR", "pL", "qZ", "qR", "qL", "pZ0", "pZ1", "pZ2", "pZ3", "pRf", "pLf", "cR", "cL",
-    "eR", "eL", "dh0", "dh1", "dh2", "dh3", "hid", "res", "m1R", "m1L", "m2R", "m2L", "m3R", "m3L",
-    "mZ0", "mZ1", "z0", "z1", "z2", "z3", "p1R", "p1L", "p2R", "p2L", "p3R", "p3L", "fq0", "fq1", "fp",
+    "xe", "seg", "pR", "pL", "pZ0", "pZ1", "pZ2", "pZ3", "pRf", "pLf", "dh0", "dh1", "dh2", "dh3",
+    "hid", "res", "z0", "z1", "z2", "z3", "p1R", "p1L", "p2R", "p2L", "p3R", "p3L", "fp", "qZ_0",
+    "qZ_1", "qR_0", "qR_1", "qL_0", "qL_1", "cR_0", "cR_1", "cL_0", "cL_1", "eR_0", "eR_1", "eL_0",
+    "eL_1", "m1R_0", "m1R_1", "m1L_0", "m1L_1", "m2R_0", "m2R_1", "m2L_0", "m2L_1", "m3R_0",
+    "m3R_1", "m3L_0", "m3L_1", "mZ_0", "mZ_1", "fq_0", "fq_1",
 )
 LOADS = (
-    "wq", "wg", "wp", "xs", "xf", "cot", "sf", "sb", "sg", "sq", "sp", "oq0", "oq1", "op", "og",
+    "wq", "wg", "wp", "xs", "xf", "cot", "sf", "sb", "sg", "sq", "sp",
 )
 
 
@@ -37,9 +39,9 @@
 
 def kernel(
     n_blk, xf_in, xs_in, xe_in, cot_in, sf_in, sb_in, qkv_in, gain_in, proj_in, sg_in, sq_in, sp_in,
-    out_h, out_g, out_q, out_p,
+    out_h, out_q, out_p,
     Wq, Wp, Gq, Gp, RQ, RPZ, RPX, X, XE, COT, HID, DH, DN, NS, ACC, PR, ATTN, ATT_T, PROBS, DP, DATT, DACC,
-    MASK, GK, GV, INV, CO, GG, SEGI, SEG, GN, SG, SQ, SP, FQ, FP, go, send_sem, recv_sem, load_sem,
+    MASK, GK, GV, INV, CO, GG, SEGI, SEG, GN, SG, SQ, SP, go, turn, send_sem, recv_sem, load_sem,
 ):
     T, D = COT.shape
     C = Wq.shape[1] - PAD
@@ -48,6 +50,7 @@
     HD = A // HEADS
     H2 = A // 2
     scale = HD ** (-0.5)
+    QR = 48 if (C + PAD) % 48 == 0 else 16
 
     b, f = lax.axis_index("blk"), lax.axis_index("fsdp")
     z, x = lax.div(f, 4), lax.rem(f, 4)
@@ -79,6 +82,24 @@
 
     def arrived(name, dst):
         remote(name, dst, dst, right).wait_recv()
+
+    cut = (C + PAD) // QR // 2 * QR
+    spans = ((0, cut), (cut, C + PAD))
+    parts = (pl.ds(0, cut), pl.ds(cut, C + PAD - cut))
+
+    def send_part(name, k, src, dst, device):
+        send(f"{name}_{k}", src.at[parts[k]], dst.at[parts[k]], device)
+
+    def send_both(name, src, dst, device):
+        for k in range(2):
+            send_part(name, k, src, dst, device)
+
+    def arrived_part(name, k, dst):
+        arrived(f"{name}_{k}", dst.at[parts[k]])
+
+    def arrived_both(name, dst):
+        for k in range(2):
+            arrived_part(name, k, dst)
 
     loads = {}
 
@@ -115,27 +136,35 @@
     loads["wg"].wait()
     loads["sf"].wait()
     loads["sb"].wait()
-    loads["wp"].wait()
+    SEG[0, 0] = jnp.broadcast_to(SEGI[0].astype(F32), (8, T))
+    SEG[0, 1] = jnp.broadcast_to(SEGI[1].astype(F32), (8, T))
     loads["wq"].wait()
     Wq[own, C : C + PAD, 0:C] = jnp.broadcast_to(GN[...].astype(F32), (PAD, C)).astype(BF16)
     Wq[own, C : C + PAD, C:Q] = jnp.zeros((PAD, Q - C), BF16)
-    SEG[0, 0] = jnp.broadcast_to(SEGI[0].astype(F32), (8, T))
-    SEG[0, 1] = jnp.broadcast_to(SEGI[1].astype(F32), (8, T))
+    loads["wp"].wait()
     pl.semaphore_wait(barrier, 5)
 
     send("xe", xe_in, XE, prev)
     send("seg", SEG.at[0], SEG.at[1], prev)
 
-    @pl.when(odd == 1)
+    def gather_starts():
+        copies = [
+            remote("pR", Wp.at[own], Wp.at[own], right),
+            remote("pL", Wp.at[own], Wp.at[own], left),
+        ]
+        for name, device in (("qZ", across), ("qR", right)):
+            for k in range(2):
+                piece = Wq.at[own, parts[k]]
+                copies.append(remote(f"{name}_{k}", piece, piece, device))
+        return copies
+
+    first_copies = gather_starts()
+    started.extend(first_copies)
+
+    @pl.when(odd == 0)
     def _():
-        pl.semaphore_wait(go, 1)
-
-    send("pR", Wp.at[own], Wp.at[own], right)
-    send("pL", Wp.at[own], Wp.at[own], left)
-    send("qZ", Wq.at[own], Wq.at[own], across)
-    send("qR", Wq.at[own], Wq.at[own], right)
-    send("qL", Wq.at[own], Wq.at[own], left)
-    send("pZ0", Wp.at[own], Wp.at[own], across)
+        for copy in first_copies:
+            copy.start()
 
     def make_mask(place, kind, slot):
         row = jnp.broadcast_to(SEG[place, kind, 0:1, :], (T, T))
@@ -250,40 +279,55 @@
     make_mask(1, 1, 2)
     make_mask(1, 0, 3)
 
+    @pl.when(odd == 1)
+    def _():
+        pl.semaphore_wait(go, 1)
+        for copy in first_copies:
+            copy.start()
+
+    arrived_part("qZ", 0, Wq.at[oz])
+    send_part("cL", 0, Wq.at[oz], Wq.at[oz], left)
+    send_part("cR", 0, Wq.at[oz], Wq.at[oz], right)
+    send("pZ0", Wp.at[own], Wp.at[own], across)
     arrived("pR", Wp.at[jL])
     send("pRf", Wp.at[jL, pl.ds(0, H2)], Wp.at[jL, pl.ds(0, H2)], right)
     send("pZ1", Wp.at[jL], Wp.at[jL], across)
     arrived("pL", Wp.at[jR])
     send("pLf", Wp.at[jR, pl.ds(H2, H2)], Wp.at[jR, pl.ds(H2, H2)], left)
     send("pZ2", Wp.at[jR], Wp.at[jR], across)
-    arrived("qZ", Wq.at[oz])
-    send("cR", Wq.at[oz], Wq.at[oz], right)
-    send("cL", Wq.at[oz], Wq.at[oz], left)
+    arrived_part("qZ", 1, Wq.at[oz])
+    send_part("cL", 1, Wq.at[oz], Wq.at[oz], left)
+    send_part("cR", 1, Wq.at[oz], Wq.at[oz], right)
+    send_both("qL", Wq.at[own], Wq.at[own], left)
+    arrived_part("qR", 0, Wq.at[jL])
+    send_part("eR", 0, Wq.at[jL], Wq.at[jL], right)
     arrived("xe", XE)
     rms(read_e, 2)
     project_piece(own)
+    arrived_part("qR", 1, Wq.at[jL])
+    send_part("eR", 1, Wq.at[jL], Wq.at[jL], right)
     arrived("pRf", Wp.at[jF, pl.ds(0, H2)])
     arrived("pLf", Wp.at[jF, pl.ds(H2, H2)])
     send("pZ3", Wp.at[jF], Wp.at[jF], across)
-    arrived("qR", Wq.at[jL])
-    send("eR", Wq.at[jL], Wq.at[jL], right)
     project_piece(oz)
     project_piece(jL)
-    arrived("qL", Wq.at[jR])
+    arrived_part("cL", 0, Wq.at[ozR])
+    send_part("eL", 0, Wq.at[ozR], Wq.at[ozR], left)
+    arrived_both("qL", Wq.at[jR])
     project_piece(jR)
+    arrived_part("cL", 1, Wq.at[ozR])
+    send_part("eL", 1, Wq.at[ozR], Wq.at[ozR], left)
+
+    @pl.when(odd == 0)
+    def _():
+        pl.semaphore_signal(go, inc=1, device_id=following, device_id_type=MESH)
+
     d_att_piece(own)
     d_att_piece(jL)
     d_att_piece(jR)
     d_att_piece(jF)
-    arrived("cL", Wq.at[ozR])
-    send("eL", Wq.at[ozR], Wq.at[ozR], left)
-
-    @pl.when(odd == 0)
-    def _():
-        pl.semaphore_signal(go, inc=1, device_id=following, device_id_type=MESH)
-
     project_piece(ozR)
-    arrived("cR", Wq.at[ozL])
+    arrived_both("cR", Wq.at[ozL])
     project_piece(ozL)
     arrived("pZ0", Wp.at[oz])
     d_att_piece(oz)
@@ -291,9 +335,9 @@
     d_att_piece(ozL)
     arrived("pZ2", Wp.at[ozR])
     d_att_piece(ozR)
-    arrived("eR", Wq.at[jF])
+    arrived_both("eR", Wq.at[jF])
     project_piece(jF)
-    arrived("eL", Wq.at[ozF])
+    arrived_both("eL", Wq.at[ozF])
     project_piece(ozF)
     PR[0] = ACC[0].astype(BF16)
     PR[1] = ACC[1].astype(BF16)
@@ -383,8 +427,6 @@
 
         lax.fori_loop(0, count, step, 0)
 
-    QR = 48 if (C + PAD) % 48 == 0 else 16
-
     def add_q(j, slots, first=0, last=C + PAD):
         def work(k):
             rows = pl.ds(pl.multiple_of(first + k * QR, 16), QR)
@@ -405,36 +447,55 @@
 
         each(size // 16, work)
 
+    result_copy = remote("res", HID, out_h, following)
+    started.append(result_copy)
+
+    def forward_two():
+        arrived("hid", HID)
+        project_all(read_h, 3, 2)
+        attention(2, 3, False, 0)
+
+        def result_piece(j, carry):
+            HID[:, cols(j)] = (HID[:, cols(j)].astype(F32) + dot(ATTN[...], Wp[j])).astype(BF16)
+            return carry
+
+        lax.fori_loop(0, 8, result_piece, 0)
+        result_copy.start()
+
     each(2, lambda k: grad_qkv(at(z + k, x + 2)))
-    send("m1R", Gq.at[jF], RQ.at[0], right)
-    send("m1L", Gq.at[ozF], RQ.at[1], left)
+
+    @pl.when(odd == 0)
+    def _():
+        pl.semaphore_wait(turn, 1)
+
+    send_both("m1R", Gq.at[jF], RQ.at[0], right)
+    send_both("m1L", Gq.at[ozF], RQ.at[1], left)
+    each(2, lambda k: grad_qkv(at(z + k, x + 1 + 2 * k)))
     each(4, lambda k: grad_proj(at(z_send, k)))
     for q, off in enumerate((2, 1, 3, 0)):
         send(f"z{q}", Gp.at[at(z_send, x + off)], RPZ.at[q], across)
-    each(2, lambda k: grad_qkv(at(z + 1 + k, x + 1 + 2 * k)))
-    send("m2R", Gq.at[ozR], RQ.at[2], right)
-    send("m2L", Gq.at[jL], RQ.at[3], left)
+    for k in range(2):
+        arrived_part("m1R", k, RQ.at[0])
+        add_q(jR, (0,), *spans[k])
+        send_part("m3R", k, Gq.at[jR], RQ.at[4], right)
+        arrived_part("m1L", k, RQ.at[1])
+        add_q(ozL, (1,), *spans[k])
+        send_part("m3L", k, Gq.at[ozL], RQ.at[5], left)
+        if k == 0:
+            each(2, lambda k: grad_qkv(at(z + 1 + k, x + 1 + 2 * k)))
+    for k in range(2):
+        send_part("m2R", k, Gq.at[ozR], RQ.at[2], right)
+        send_part("m2L", k, Gq.at[jL], RQ.at[3], left)
+
+    @pl.when(odd == 1)
+    def _():
+        pl.semaphore_signal(turn, inc=1, device_id=prev, device_id_type=MESH)
+
+    pl.when(odd == 1)(forward_two)
     pl.when(odd == 1)(forward_one)
-    each(2, lambda k: grad_qkv(at(z + k, x + 1 + 2 * k)))
     each(2, lambda k: grad_qkv(at(z + k, x)))
     each(4, lambda k: grad_proj(at(z_keep, k)))
-    arrived("m1R", RQ.at[0])
-    add_q(jR, (0,))
-    send("m3R", Gq.at[jR], RQ.at[4], right)
-    arrived("m1L", RQ.at[1])
-    add_q(ozL, (1,))
-    send("m3L", Gq.at[ozL], RQ.at[5], left)
-
-    arrived("hid", HID)
-    project_all(read_h, 3, 1)
-    attention(1, 3, False, 0)
-
-    def result_piece(j, carry):
-        HID[:, cols(j)] = (HID[:, cols(j)].astype(F32) + dot(ATTN[...], Wp[j])).astype(BF16)
-        return carry
-
-    lax.fori_loop(0, 8, result_piece, 0)
-    send("res", HID, out_h, following)
+    pl.when(odd == 0)(forward_two)
 
     kF, kR, kL, kO = (at(z_keep, x + off) for off in (2, 1, 3, 0))
     top, low = pl.ds(0, H2), pl.ds(H2, H2)
@@ -448,16 +509,14 @@
     arrived("z2", RPZ.at[2])
     add_p(kL, 0, A, (RPZ.at[2],))
     send("p2L", Gp.at[kL, top], RPX.at[3], left)
-    arrived("m2R", RQ.at[2])
-    arrived("m2L", RQ.at[3])
-    arrived("m3R", RQ.at[4])
-    arrived("m3L", RQ.at[5])
     j_send, j_keep = at(z_send, x), at(z_keep, x)
-    cut = (C + PAD) // QR // 2 * QR
-    part0, part1 = pl.ds(0, cut), pl.ds(cut, C + PAD - cut)
-    add_q(j_send, (2 + odd, 5 - odd))
-    send("mZ0", Gq.at[j_send, part0], RQ.at[6, part0], across)
-    send("mZ1", Gq.at[j_send, part1], RQ.at[6, part1], across)
+    for k in range(2):
+        arrived_part("m2R", k, RQ.at[2])
+        arrived_part("m2L", k, RQ.at[3])
+        arrived_part("m3R", k, RQ.at[4])
+        arrived_part("m3L", k, RQ.at[5])
+        add_q(j_send, (2 + odd, 5 - odd), *spans[k])
+        send_part("mZ", k, Gq.at[j_send], RQ.at[6], across)
     arrived("p1R", RPX.at[0])
     add_p(kR, 0, H2, (RPX.at[0],))
     send("p3R", Gp.at[kR, top], RPX.at[4], right)
@@ -472,30 +531,24 @@
     arrived("p3L", RPX.at[5])
     add_p(kO, 0, H2, (RPZ.at[3, top], RPX.at[4], RPX.at[3]))
     add_p(kO, H2, H2, (RPZ.at[3, low], RPX.at[2], RPX.at[5]))
-    send("fp", Gp.at[kO], FP, following)
-    arrived("mZ0", RQ.at[6, part0])
-    add_q(j_keep, (6,), 0, cut)
-    send("fq0", Gq.at[j_keep, part0], FQ.at[part0], following)
-    arrived("mZ1", RQ.at[6, part1])
-    add_q(j_keep, (6,), cut)
-    send("fq1", Gq.at[j_keep, part1], FQ.at[part1], following)
-
-    arrived("fp", FP)
-    SP[...] = FP[...].astype(F32)
-    load("op", SP, out_p)
-    arrived("fq0", FQ.at[part0])
-    SQ[0:cut, :] = FQ[0:cut, :].astype(F32)
-    load("oq0", SQ.at[part0], out_q.at[part0])
-    arrived("fq1", FQ.at[part1])
-    SG[...] = FQ[C : C + PAD, 0:C].astype(F32)[0:1, :]
-    load("og", SG, out_g)
-    SQ[cut:C, :] = FQ[cut:C, :].astype(F32)
-    load("oq1", SQ.at[pl.ds(cut, C - cut)], out_q.at[pl.ds(cut, C - cut)])
+    send("fp", Gp.at[kO], out_p, following)
+    for k in range(2):
+        arrived_part("mZ", k, RQ.at[6])
+        add_q(j_keep, (6,), *spans[k])
+        send_part("fq", k, Gq.at[j_keep], out_q, following)
+
     arrived("res", out_h)
-    for name in ("op", "oq0", "og", "oq1"):
-        loads[name].wait()
+    arrived("fp", out_p)
+    arrived_both("fq", out_q)
     for copy in started:
         copy.wait_send()
+
+
+def widen(hidden_ref, q_ref, g_ref, p_ref, out_h, out_g, out_q, out_p):
+    out_h[...] = hidden_ref[...]
+    out_g[...] = g_ref[...].astype(F32)[0:1, : out_g.shape[1]]
+    out_q[...] = q_ref[...].astype(F32)
+    out_p[...] = p_ref[...].astype(F32)
 
 
 def body(
@@ -517,21 +570,20 @@
         V((T, A), BF16), V((T, A), F32), V((4, T, T), F32), V((T, HD), F32), V((T, HD), F32),
         V((4, T, 128), F32), V((T, 128), F32), V((8, 8, C), F32), V((2, 1, T), jnp.int32),
         V((2, 2, 8, T), F32), V((1, C), BF16), V((1, C), F32), V((C, Q), F32), V((A, C), F32),
-        V((C + PAD, Q), BF16), V((A, C), BF16), pltpu.SemaphoreType.REGULAR,
+        pltpu.SemaphoreType.REGULAR, pltpu.SemaphoreType.REGULAR,
         pltpu.SemaphoreType.DMA((len(MESSAGES),)),
         pltpu.SemaphoreType.DMA((len(MESSAGES),)),
         pltpu.SemaphoreType.DMA((len(LOADS),)),
     ]
-    hidden, new_g, new_q, new_p = pl.pallas_call(
+    hidden, new_q, new_p = pl.pallas_call(
         functools.partial(kernel, n_blk),
         out_shape=(
             jax.ShapeDtypeStruct((T, D), BF16),
-            jax.ShapeDtypeStruct((1, C), F32),
-            jax.ShapeDtypeStruct((C, Q), F32),
-            jax.ShapeDtypeStruct((A, C), F32),
+            jax.ShapeDtypeStruct((C + PAD, Q), BF16),
+            jax.ShapeDtypeStruct((A, C), BF16),
         ),
         in_specs=[anywhere] * 12,
-        out_specs=(anywhere,) * 4,
+        out_specs=(anywhere,) * 3,
         scratch_shapes=scratch,
         compiler_params=pltpu.CompilerParams(
             collective_id=0, has_side_effects=True, vmem_limit_bytes=VMEM_LIMIT
@@ -541,6 +593,30 @@
         x_forward, x_saved, x_earlier, cotangent, seg_forward, seg_backward, qkv[0], gain, proj[0],
         sum_gain, sum_qkv[0], sum_proj[0],
     )
+    n = 4
+    hidden, new_g, new_q, new_p = pl.pallas_call(
+        widen,
+        grid=(n,),
+        out_shape=(
+            jax.ShapeDtypeStruct((T, D), BF16),
+            jax.ShapeDtypeStruct((1, C), F32),
+            jax.ShapeDtypeStruct((C, Q), F32),
+            jax.ShapeDtypeStruct((A, C), F32),
+        ),
+        in_specs=[
+            pl.BlockSpec((T // n, D), lambda i: (i, 0)),
+            pl.BlockSpec((C // n, Q), lambda i: (i, 0)),
+            pl.BlockSpec((PAD, Q), lambda i: (C // PAD, 0)),
+            pl.BlockSpec((A // n, C), lambda i: (i, 0)),
+        ],
+        out_specs=(
+            pl.BlockSpec((T // n, D), lambda i: (i, 0)),
+            pl.BlockSpec((1, C), lambda i: (0, 0)),
+            pl.BlockSpec((C // n, Q), lambda i: (i, 0)),
+            pl.BlockSpec((A // n, C), lambda i: (i, 0)),
+        ),
+        name="widen",
+    )(hidden, new_q, new_q, new_p)
     return hidden, new_g, new_q[None], new_p[None]
 
 

time: 195 us -> 180 us (0.923)
  Pallas kernels: 188 us -> 179 us
  local copies, waits for them, and re-layouts: 5.95 us -> 0 us
    pallas_call x1, Pallas kernels: 188 us -> 175 us  [body(): pl.pallas_call(functools.partial(kernel, n_blk), out_shape=(jax.ShapeDtyp...]
    unnamed x10 -> x0, local copies, waits for them, and re-layouts: 5.95 us -> none
    pallas_call x0 -> x1, Pallas kernels: none -> 4.59 us  [body(): pl.pallas_call(widen, grid=(n,), out_shape=(jax.ShapeDtypeStruct((T, D),...]
where the time goes in v2:
time: 180 us
  Pallas kernels  179 us (99%)
    pallas_call x1, Pallas kernels, body(): pl.pallas_call(functools.partial(kernel, n_blk), out_shape=(jax.ShapeDtyp...  175 us
    pallas_call x1, Pallas kernels, body(): pl.pallas_call(widen, grid=(n,), out_shape=(jax.ShapeDtypeStruct((T, D),...  4.59 us

profile of v2, /device:TPU:0, one launch (start us, length us, event | category | flops | bytes accessed | tf_op | source)
XLA Modules:
  0.0 179.8 jit_solution(4571784471301484025)
XLA Ops:
  0.6 174.6 %two_steps.1 = (bf16[256,4096]{1,0:T(8,128)(2,1)}, bf16[528,768]{1,0:T(8,128)(2,1)}, bf16[512,512]{1,0:T(8,128)(2,1)}) custom-call(bf16[256,4096]{1,0:T(8,128)(2,1)} %xf_in.1, bf16[256,4096]{1,0:T(8,128)(2,1)} %xs_in.1, bf16[256,4096]{1,0:T(8,128)(2,1)} %xe_in.1, bf16[256,4096]{1,0:T(8,128)(2,1)} %cot_in.1, s32[1,256]{1,0:T(1,128)} %sf_in.1, ...), custom_call_target="tpu_custom_call" | custom-call | tf_op jit(solution)/shard_map/two_steps/pallas_call | solution.py:578
  175.3 4.6 %widen.1 = (bf16[256,4096]{1,0:T(8,128)(2,1)}, f32[1,512]{1,0:T(1,128)}, f32[512,768]{1,0:T(8,128)}, f32[512,512]{1,0:T(8,128)}) custom-call(bf16[256,4096]{1,0:T(8,128)(2,1)} %get-tuple-element.11.hidden_ref, bf16[528,768]{1,0:T(8,128)(2,1)} %get-tuple-element.12.q_ref.g_ref, bf16[528,768]{1,0:T(8,128)(2,1)} %get-tuple-element.12.q_ref.g_ref, ...), custom_call_target="tpu_custom_call" | custom-call | tf_op jit(solution)/shard_map/widen/pallas_call | solution.py:597

commit v3 on v2

--- a/solution.py
+++ b/solution.py
@@ -360,17 +360,26 @@
     total = lax.fori_loop(0, 8, scaled_piece, jnp.zeros((T, 128), F32))
     inv = INV[0]
     CO[...] = inv * inv * inv * (jnp.sum(total, axis=1, keepdims=True) * (1.0 / D))
+    dx_copies = []
     for k in range(4):
-        rows = slice(k * (T // 4), (k + 1) * (T // 4))
-
-        def dx_piece(j, carry):
-            v = X[0, rows, cols(j)].astype(F32)
-            d_wide = wide(INV[0, rows, :]) * DN[j, rows, :] - v * wide(CO[rows, :])
-            X[0, rows, cols(j)] = (COT[rows, cols(j)].astype(F32) + d_wide).astype(BF16)
-            return carry
-
-        lax.fori_loop(0, 8, dx_piece, 0)
-        send(f"dh{k}", X.at[0, pl.ds(k * (T // 4), T // 4)], DH.at[pl.ds(k * (T // 4), T // 4)], prev)
+        rows = pl.ds(k * (T // 4), T // 4)
+        dx_copies.append(remote(f"dh{k}", X.at[0, rows], DH.at[rows], prev))
+    started.extend(dx_copies)
+
+    def send_dx():
+        for k in range(4):
+            rows = slice(k * (T // 4), (k + 1) * (T // 4))
+
+            def dx_piece(j, carry):
+                v = X[0, rows, cols(j)].astype(F32)
+                d_wide = wide(INV[0, rows, :]) * DN[j, rows, :] - v * wide(CO[rows, :])
+                X[0, rows, cols(j)] = (COT[rows, cols(j)].astype(F32) + d_wide).astype(BF16)
+                return carry
+
+            lax.fori_loop(0, 8, dx_piece, 0)
+            dx_copies[k].start()
+
+    pl.when(odd == 0)(send_dx)
 
     hidden_copy = remote("hid", X.at[1], HID, prev)
     started.append(hidden_copy)
@@ -470,6 +479,7 @@
 
     send_both("m1R", Gq.at[jF], RQ.at[0], right)
     send_both("m1L", Gq.at[ozF], RQ.at[1], left)
+    pl.when(odd == 1)(send_dx)
     each(2, lambda k: grad_qkv(at(z + k, x + 1 + 2 * k)))
     each(4, lambda k: grad_proj(at(z_send, k)))
     for q, off in enumerate((2, 1, 3, 0)):

time: 180 us -> 179 us (level)
  no operation moved by 1% of the time
where the time goes in v3:
time: 179 us
  Pallas kernels  178 us (99%)
    pallas_call x1, Pallas kernels, body(): pl.pallas_call(functools.partial(kernel, n_blk), out_shape=(jax.ShapeDtyp...  174 us
    pallas_call x1, Pallas kernels, body(): pl.pallas_call(widen, grid=(n,), out_shape=(jax.ShapeDtypeStruct((T, D),...  4.59 us

profile of v3, /device:TPU:0, one launch (start us, length us, event | category | flops | bytes accessed | tf_op | source)
XLA Modules:
  0.0 178.8 jit_solution(5060816277124349330)
XLA Ops:
  0.6 173.5 %two_steps.1 = (bf16[256,4096]{1,0:T(8,128)(2,1)}, bf16[528,768]{1,0:T(8,128)(2,1)}, bf16[512,512]{1,0:T(8,128)(2,1)}) custom-call(bf16[256,4096]{1,0:T(8,128)(2,1)} %xf_in.1, bf16[256,4096]{1,0:T(8,128)(2,1)} %xs_in.1, bf16[256,4096]{1,0:T(8,128)(2,1)} %xe_in.1, bf16[256,4096]{1,0:T(8,128)(2,1)} %cot_in.1, s32[1,256]{1,0:T(1,128)} %sf_in.1, ...), custom_call_target="tpu_custom_call" | custom-call | tf_op jit(solution)/shard_map/two_steps/pallas_call | solution.py:588
  174.2 4.6 %widen.1 = (bf16[256,4096]{1,0:T(8,128)(2,1)}, f32[1,512]{1,0:T(1,128)}, f32[512,768]{1,0:T(8,128)}, f32[512,512]{1,0:T(8,128)}) custom-call(bf16[256,4096]{1,0:T(8,128)(2,1)} %get-tuple-element.11.hidden_ref, bf16[528,768]{1,0:T(8,128)(2,1)} %get-tuple-element.12.q_ref.g_ref, bf16[528,768]{1,0:T(8,128)(2,1)} %get-tuple-element.12.q_ref.g_ref, ...), custom_call_target="tpu_custom_call" | custom-call | tf_op jit(solution)/shard_map/widen/pallas_call | solution.py:607

commit v4 on v3

--- a/solution.py
+++ b/solution.py
@@ -471,13 +471,14 @@
         lax.fori_loop(0, 8, result_piece, 0)
         result_copy.start()
 
-    each(2, lambda k: grad_qkv(at(z + k, x + 2)))
+    grad_qkv(jF)
 
     @pl.when(odd == 0)
     def _():
         pl.semaphore_wait(turn, 1)
 
     send_both("m1R", Gq.at[jF], RQ.at[0], right)
+    grad_qkv(ozF)
     send_both("m1L", Gq.at[ozF], RQ.at[1], left)
     pl.when(odd == 1)(send_dx)
     each(2, lambda k: grad_qkv(at(z + k, x + 1 + 2 * k)))

time: 179 us -> 179 us (level)
  no operation moved by 1% of the time
where the time goes in v4:
time: 179 us
  Pallas kernels  178 us (99%)
    pallas_call x1, Pallas kernels, body(): pl.pallas_call(functools.partial(kernel, n_blk), out_shape=(jax.ShapeDtyp...  174 us
    pallas_call x1, Pallas kernels, body(): pl.pallas_call(widen, grid=(n,), out_shape=(jax.ShapeDtypeStruct((T, D),...  4.59 us

profile of v4, /device:TPU:0, one launch (start us, length us, event | category | flops | bytes accessed | tf_op | source)
XLA Modules:
  0.0 178.8 jit_solution(631006805333145126)
XLA Ops:
  0.6 173.5 %two_steps.1 = (bf16[256,4096]{1,0:T(8,128)(2,1)}, bf16[528,768]{1,0:T(8,128)(2,1)}, bf16[512,512]{1,0:T(8,128)(2,1)}) custom-call(bf16[256,4096]{1,0:T(8,128)(2,1)} %xf_in.1, bf16[256,4096]{1,0:T(8,128)(2,1)} %xs_in.1, bf16[256,4096]{1,0:T(8,128)(2,1)} %xe_in.1, bf16[256,4096]{1,0:T(8,128)(2,1)} %cot_in.1, s32[1,256]{1,0:T(1,128)} %sf_in.1, ...), custom_call_target="tpu_custom_call" | custom-call | tf_op jit(solution)/shard_map/two_steps/pallas_call | solution.py:589
  174.2 4.6 %widen.1 = (bf16[256,4096]{1,0:T(8,128)(2,1)}, f32[1,512]{1,0:T(1,128)}, f32[512,768]{1,0:T(8,128)}, f32[512,512]{1,0:T(8,128)}) custom-call(bf16[256,4096]{1,0:T(8,128)(2,1)} %get-tuple-element.11.hidden_ref, bf16[528,768]{1,0:T(8,128)(2,1)} %get-tuple-element.12.q_ref.g_ref, bf16[528,768]{1,0:T(8,128)(2,1)} %get-tuple-element.12.q_ref.g_ref, ...), custom_call_target="tpu_custom_call" | custom-call | tf_op jit(solution)/shard_map/widen/pallas_call | solution.py:608
